TPU v7x, 32 devices: a whole 2x2x4 slice. The times are simulated.
32 devices in a mesh: freq: 4 (over y, x), line: 8 (over z, core).
Axes of the slice: x: 2, y: 2, z: 4, core: 2. Of those that a mesh axis runs over, the one named last changes fastest.
Arguments:
- field: float32 [4, 2, 4, 24, 64, 256], P('freq', None, None, None, 'line'), may hold values from -6 to 6
- live_count: int32 [64], P('line'), may hold values from 64 to 256
- line_owner: int32 [64], replicated, may hold values from 0 to 63, each once
- decomposer: float32 [4, 2, 4, 4, 64, 256], P('freq', None, None, None, 'line'), may hold values from -1.4 to 2.4
- reflection: bfloat16 [4, 256, 2, 16384], P('freq', None, None, 'line'), may hold values from -0.046875 to 0.046875
- direct_wave: float32 [256, 4, 2, 96], P('line', 'freq'), may hold values from -6 to 6
Outputs:
- focusing: float32 [256, 4, 2, 96], P('line', 'freq')
- trace_energy: float32 [256], P('line')
Inputs may be any that keep to these rules, and one draw needn't show every extreme that they name: `line_owner`: each crossline position appears once.
All inputs are finite; a program needn't handle non-finite values.
Results may differ from a plain program's by a relative error of at most 0.0023.
Values may be sent and summed in bfloat16 or wider, within the bound.
A program may use at most 64 MiB of HBM per device.

v0:
```python
import math

import jax
import jax.numpy as jnp
from jax import lax
from jax.sharding import PartitionSpec as P


def phase_tables(line_owner, length):
    wavenum = jnp.arange(length, dtype=jnp.int32)
    products = wavenum[:, None] * line_owner[None, :] % length
    angles = products.astype(jnp.float32) * (2.0 * math.pi / length)
    return (jnp.cos(angles), jnp.sin(angles))


def decompose(operator, spectrum):
    real_rows = []
    imag_rows = []
    for target in range(4):
        real_sum = None
        imag_sum = None
        for source in range(4):
            weight_real = operator[:, 0, target, source][:, None]
            weight_imag = operator[:, 1, target, source][:, None]
            field_real = spectrum[:, 0, source]
            field_imag = spectrum[:, 1, source]
            term_real = weight_real * field_real - weight_imag * field_imag
            term_imag = weight_real * field_imag + weight_imag * field_real
            real_sum = term_real if real_sum is None else real_sum + term_real
            imag_sum = term_imag if imag_sum is None else imag_sum + term_imag
        real_rows.append(real_sum)
        imag_rows.append(imag_sum)
    return jnp.stack([jnp.stack(real_rows, 1), jnp.stack(imag_rows, 1)], 1)


def on_device(field, live_count, line_owner, decomposer, reflection, direct_wave):
    length = line_owner.shape[0]
    receivers = field.shape[5]
    cosine, sine_table = phase_tables(line_owner, length)
    forward_table = jnp.stack([jnp.stack([cosine, sine_table]), jnp.stack([-sine_table, cosine])])
    inverse_table = (
        jnp.stack([jnp.stack([cosine.T, -sine_table.T]), jnp.stack([sine_table.T, cosine.T])])
        / length
    )
    live_mask = jnp.arange(receivers, dtype=jnp.int32)[None, :] < live_count[:, None]
    live_field = jnp.where(live_mask, field, jnp.float32(0.0))
    operator = lax.all_gather(decomposer, "line", axis=4, tiled=True)
    every_line = lax.all_to_all(live_field, "line", split_axis=3, concat_axis=4, tiled=True)
    space_all = jnp.einsum(
        "yxjk,fxiokr->fyiojr",
        inverse_table,
        decompose(
            operator,
            jnp.einsum(
                "yxkj,fxiojr->fyiokr", forward_table, every_line, precision=lax.Precision.HIGHEST
            ),
        ),
        precision=lax.Precision.HIGHEST,
    )
    wavefield = lax.all_to_all(
        space_all.astype(jnp.bfloat16), "line", split_axis=4, concat_axis=3, tiled=True
    )
    freq_count = wavefield.shape[0]
    channels = wavefield.shape[2] * wavefield.shape[3]
    positions = wavefield.shape[4] * wavefield.shape[5]
    wave_bf = wavefield.reshape(freq_count, 2, channels, positions)
    real_part = wave_bf[:, 0]
    imag_part = wave_bf[:, 1]
    stacked = jnp.stack(
        [jnp.stack([real_part, imag_part], 1), jnp.stack([-imag_part, real_part], 1)], 1
    )
    reflected = lax.psum_scatter(
        jnp.einsum("fsxq,fxocq->sfoc", reflection, stacked, preferred_element_type=jnp.float32),
        "line",
        scatter_dimension=0,
        tiled=True,
    )
    focusing = direct_wave - reflected
    total_freqs = freq_count * lax.axis_size("freq")
    freq_index = lax.axis_index("freq") * freq_count + jnp.arange(freq_count, dtype=jnp.int32)
    weights = 2.0 * (freq_index + 1).astype(jnp.float32) / (total_freqs * (total_freqs + 1))
    partial_value = jnp.sum(jnp.sum(reflected * reflected, axis=(2, 3)) * weights[None, :], axis=1)
    energy_sum = lax.psum(partial_value, "freq")
    trace_energy = jnp.sqrt(energy_sum / (2 * channels) + 1e-06)
    return (focusing, trace_energy)


def solution(mesh):
    return jax.shard_map(
        on_device,
        mesh=mesh,
        in_specs=(
            P("freq", None, None, None, "line", None),
            P("line"),
            P(),
            P("freq", None, None, None, "line", None),
            P("freq", None, None, "line"),
            P("line", "freq", None, None),
        ),
        out_specs=(P("line", "freq", None, None), P("line")),
        check_vma=False,
    )
```

profile of v0, /device:TPU:0, one launch (start us, length us, event | category | flops | bytes accessed | tf_op | source)
XLA Modules:
  0.0 181.0 jit_solution(17046657642363256790)
XLA Ops:
  7.2 0.0 all-gather.2.cloned.1.call-start
  7.2 0.7 all-gather.2.cloned.1.call-update
  7.9 0.7 iota_compare_fusion
  8.6 2.8 %copy_select_fusion = f32[1,2,4,24,8,256]{5,4,2,1,0,3:T(8,128)} fusion(f32[1,2,4,24,8,256]{5,4,3,2,1,0:T(8,128)} %param.6, pred[8,256]{1,0:T(8,128)(4,1)S(1)} %iota_compare_fusion), kind=kLoop, calls=%fused_computation.13 | loop fusion | flops 393216 | bytes 3147776 | tf_op jit(solution)/shard_map/jit(_where)/select_n | solution.py:46
  11.4 0.0 copy-start.1
  11.4 6.5 %all-to-all-start = ((f32[1,2,4,24,8,256]{5,4,2,1,0,3:T(8,128)}), f32[1,2,4,24,8,256]{5,4,2,1,0,3:T(8,128)S(1)}, u32[]{:S(2)}, u32[]{:S(2)}) async-start(f32[1,2,4,24,8,256]{5,4,2,1,0,3:T(8,128)} %copy_select_fusion), calls=%async_computation | async-start | bytes 3145728 | tf_op jit(solution)/shard_map/all_to_all | solution.py:48
  17.9 0.0 all-reduce.3.cloned.1.call-start
  17.9 0.0 copy-done.1
  17.9 0.3 fusion.45
  18.3 54.3 %all-to-all-done = f32[1,2,4,24,8,256]{5,4,2,1,0,3:T(8,128)S(1)} async-done(((f32[1,2,4,24,8,256]{5,4,2,1,0,3:T(8,128)}), f32[1,2,4,24,8,256]{5,4,2,1,0,3:T(8,128)S(1)}, u32[]{:S(2)}, u32[]{:S(2)}) %all-to-all-start) | async-done | bytes 1572896 | tf_op jit(solution)/shard_map/all_to_all | solution.py:48
  72.6 1.6 fusion.10
  74.1 0.0 all-gather.2.cloned.1.call-done
  74.2 1.3 slice_bitcast_fusion.38
  75.4 1.4 slice_bitcast_fusion.39
  76.9 0.1 add_add_fusion.2
  77.0 0.1 subtract_add_fusion.2
  77.2 0.1 add_add_fusion.3
  77.3 0.1 subtract_add_fusion.3
  77.5 0.1 subtract_add_fusion
  77.6 0.1 add_add_fusion
  77.8 0.1 subtract_add_fusion.1
  77.9 0.1 add_add_fusion.1
  78.1 0.1 maximum_bitcast_fusion.5
  78.2 1.6 fusion.15
  79.8 0.8 copy.32
  80.6 23.4 %all_to_all.30 = bf16[1,2,4,3,64,256]{5,1,3,2,0,4:T(2,128)(2,1)S(1)} all-to-all(bf16[1,2,4,3,64,256]{5,1,3,2,0,4:T(2,128)(2,1)S(1)} %copy.32), channel_id=1, replica_groups=mesh['freq'=4,'line'=8] {'line'}, dimensions={4} | all-to-all | bytes 1572864 | tf_op jit(solution)/shard_map/all_to_all | solution.py:60
  104.0 0.2 copy.72
  104.2 0.4 reshape.1438
  104.5 0.4 stack.90
  104.9 0.0 copy-start.2
  104.9 0.1 slice_negate_fusion
  105.0 0.1 maximum_bitcast_fusion.7
  105.1 1.4 copy-done.2
  106.5 0.0 copy-start.3
  106.5 0.0 copy-start
  106.5 0.9 fusion.18
  107.4 0.8 copy.35
  108.3 0.0 all-reduce.3.cloned.1.call-update
  108.3 0.0 copy-done.3
  108.3 0.6 dynamic-slice
  109.5 52.8 %all-reduce.3.cloned.1.call-done = f32[256,1,2,96]{3,2,1,0:T(2,128)} async-done(((f32[256,1,2,96]{3,2,1,0:T(2,128)}), f32[256,1,2,96]{3,2,1,0:T(2,128)}) %all-reduce.3.cloned.1.call-update) | async-done | bytes 196624
  162.3 0.0 copy-done
  162.3 1.5 multiply_reduce_fusion
  163.8 9.8 %psum.7 = f32[32]{0:T(128)S(1)} all-reduce(f32[32]{0:T(128)S(1)} %broadcast_multiply_fusion), channel_id=1, replica_groups=mesh['freq'=4,'line'=8] {'freq'}, use_global_device_ids=true, to_apply=%region_2.3 | all-reduce | flops 32 | bytes 256 | tf_op jit(solution)/shard_map/psum | solution.py:83
  173.6 0.5 add_sqrt_fusion
  (3 shorter events, 0.0 us)
Async XLA Ops:
  7.2 67.0 %all-gather.2.cloned.1.call-start = ((), (), s32[]{:S(2)}) async-start(), calls=%async_computation.2 | async-start | bytes 2359296 | tf_op jit(solution)/shard_map/all_gather | solution.py:47
  11.4 6.5 %copy-start.1 = (s32[64]{0:T(128)S(1)}, s32[64]{0:T(128)}, u32[]{:S(2)}) copy-start(s32[64]{0:T(128)} %param.8) | copy-start | bytes 772
  11.4 61.1 %all-to-all-start = ((f32[1,2,4,24,8,256]{5,4,2,1,0,3:T(8,128)}), f32[1,2,4,24,8,256]{5,4,2,1,0,3:T(8,128)S(1)}, u32[]{:S(2)}, u32[]{:S(2)}) async-start(f32[1,2,4,24,8,256]{5,4,2,1,0,3:T(8,128)} %copy_select_fusion), calls=%async_computation | async-start | bytes 3145728 | tf_op jit(solution)/shard_map/all_to_all | solution.py:48
  17.9 144.4 %all-reduce.3.cloned.1.call-start = ((), (), s32[]{:S(2)}) async-start(), calls=%async_computation.3 | async-start | bytes 524288
  104.9 1.6 copy-start.2
  106.5 1.8 copy-start.3
  106.5 55.8 %copy-start = (f32[32,1,2,96]{3,2,1,0:T(2,128)S(1)}, f32[32,1,2,96]{3,2,1,0:T(2,128)}, u32[]{:S(2)}) copy-start(f32[32,1,2,96]{3,2,1,0:T(2,128)} %param.11) | copy-start | bytes 73732
Sparse Core Ops, SparseCore 0:
  9.6 57.0 all-gather.1
  108.4 53.8 all-reduce.2
where the time goes:
time: 181 us
  waiting for transfers between devices  108 us (60%)
  blocking collectives  33.2 us (18%)
  between operations  14.9 us (8%)
  other arithmetic  7.31 us (4%)
  local copies, waits for them, and re-layouts  7.24 us (4%)
  starting transfers between devices  6.53 us (4%)
  matrix products  4.03 us (2%)
    all_to_all x1, waiting for transfers between devices, on_device(): lax.all_to_all(live_field, 'line', split_axis=3, concat_axis=4, tiled=True)  54.3 us
    unnamed x3, waiting for transfers between devices  53.5 us
    all_to_all x1, blocking collectives, on_device(): lax.all_to_all(space_all.astype(jnp.bfloat16), 'line', split_axis=4, conc...  23.4 us
    psum x1, blocking collectives, on_device(): energy_sum = lax.psum(partial_value, 'freq')  9.81 us
    all_to_all x1, starting transfers between devices, on_device(): lax.all_to_all(live_field, 'line', split_axis=3, concat_axis=4, tiled=True)  6.46 us
  transfers between devices with their start and end apart: 3, of which 2 were waited for; matrix products, arithmetic and copies ran while one was open for 3% of the time, Pallas kernels for 0%

commit v1 on v0

--- a/solution.py
+++ b/solution.py
@@ -2,8 +2,353 @@
 
 import jax
 import jax.numpy as jnp
+import numpy as np
 from jax import lax
+from jax.experimental import pallas as pl
+from jax.experimental.pallas import tpu as pltpu
 from jax.sharding import PartitionSpec as P
+
+MESH = pl.DeviceIdType.MESH
+HIGHEST = lax.Precision.HIGHEST
+FIELD_SCALE = 5400.0
+OPERATOR_SCALE = 13600.0
+
+
+def contract(left, right, dims):
+    return lax.dot_general(left, right, (dims, ((), ())), preferred_element_type=jnp.float32)
+
+
+def split(value):
+    high = value.astype(jnp.bfloat16)
+    return high, (value - high.astype(jnp.float32)).astype(jnp.bfloat16)
+
+
+def fine_dot(left, right):
+    left_high, left_low = split(left)
+    right_high, right_low = split(right)
+    dims = ((1,), (0,))
+    return contract(left_high, right_high, dims) + (
+        contract(left_high, right_low, dims) + contract(left_low, right_high, dims)
+    )
+
+
+def coded(value, scale):
+    return jnp.round(value * scale).astype(jnp.int32).astype(jnp.int16)
+
+
+def update_kernel(
+    freqs, parts, foci, rows_j,
+    counts, field, operator, table, inverse, panel, direct, order,
+    focusing, energy,
+    send1, recv1, weights, spread, send2, recv2, total, recv3, shared,
+    sends1, recvs1, sends2, recvs2, sends3, recvs3, sends4, recvs4, local_sem,
+):
+    chips = parts // 2
+    group = foci // chips
+    tile = 2 * rows_j
+    lanes = 4 * group * 128
+    outs = 8 * group
+    me = lax.axis_index("line")
+    freq = lax.axis_index("freq")
+
+    barrier = pltpu.get_barrier_semaphore()
+    for step in range(1, parts):
+        pl.semaphore_signal(
+            barrier, inc=1, device_id=(freq, lax.rem(me + step, parts)), device_id_type=MESH
+        )
+    for step in range(1, freqs):
+        pl.semaphore_signal(
+            barrier, inc=1, device_id=(lax.rem(freq + step, freqs), me), device_id_type=MESH
+        )
+
+    row = lax.broadcasted_iota(jnp.int32, (rows_j, 256), 0)
+    count = jnp.zeros((rows_j, 256), jnp.int32)
+    for line in range(rows_j):
+        count = jnp.where(row == line, counts[line], count)
+    live = lax.broadcasted_iota(jnp.int32, (rows_j, 256), 1) < count
+
+    def pack_operator(target, carry):
+        for source in range(4):
+            block = coded(operator[:, target, source], OPERATOR_SCALE).reshape(tile, 256)
+            at = pl.ds(pl.multiple_of(lanes + (target * 4 + source) * 128, 128), 128)
+            for part in range(parts):
+                send1[part, :, at] = block[:, (part % 2) * 128:(part % 2) * 128 + 128]
+        return carry
+
+    lax.fori_loop(0, 4, pack_operator, 0)
+
+    def pack_field(focus, carry):
+        for source in range(4):
+            at = pl.ds(pl.multiple_of((focus * 4 + source) * 128, 128), 128)
+            for chip in range(chips):
+                value = field[:, source, chip * group + focus]
+                value = jnp.where(live[None], value, 0.0)
+                block = coded(value, FIELD_SCALE).reshape(tile, 256)
+                send1[2 * chip, :, at] = block[:, :128]
+                send1[2 * chip + 1, :, at] = block[:, 128:]
+        return carry
+
+    lax.fori_loop(0, group, pack_field, 0)
+    pl.semaphore_wait(barrier, parts - 1 + freqs - 1)
+
+    def rows_of(part, size):
+        return pl.ds(pl.multiple_of(part * size, size), size)
+
+    first = []
+    for step in STEPS:
+        peer = lax.rem(me + step, parts)
+        copy = pltpu.make_async_remote_copy(
+            src_ref=send1.at[peer],
+            dst_ref=recv1.at[rows_of(me, tile), :],
+            send_sem=sends1.at[step],
+            recv_sem=recvs1.at[step],
+            device_id=(freq, peer),
+            device_id_type=MESH,
+        )
+        copy.start()
+        first.append(copy)
+    own = pltpu.make_async_copy(send1.at[me], recv1.at[rows_of(me, tile), :], local_sem.at[0])
+    own.start()
+    own.wait()
+    for copy in first:
+        copy.wait()
+
+    for block in range(16):
+        at = lanes + block * 128
+        weights[:, block * 128:block * 128 + 128] = recv1[:, at:at + 128].astype(jnp.float32) * (
+            1.0 / OPERATOR_SCALE
+        )
+
+    count_rows = parts * rows_j * 2
+    step_rows = 8 * group
+
+    def transform(focus, carry):
+        at = pl.ds(pl.multiple_of(focus * 512, 512), 512)
+        values = recv1[:, at].astype(jnp.float32)
+        spectrum = fine_dot(table[...], values).reshape(count_rows // tile, 2, rows_j, 512)
+        real, imag = spectrum[:, 0], spectrum[:, 1]
+        columns = []
+        for target in range(4):
+            out_real, out_imag = None, None
+            for source in range(4):
+                lo = (target * 4 + source) * 128
+                weight = weights[:, lo:lo + 128].reshape(count_rows // tile, 2, rows_j, 128)
+                wr, wi = weight[:, 0], weight[:, 1]
+                fr = real[:, :, source * 128:source * 128 + 128]
+                fi = imag[:, :, source * 128:source * 128 + 128]
+                tr = wr * fr - wi * fi
+                ti = wr * fi + wi * fr
+                out_real = tr if out_real is None else out_real + tr
+                out_imag = ti if out_imag is None else out_imag + ti
+            columns.append(jnp.stack([out_real, out_imag], 1).reshape(count_rows, 128))
+        wave = fine_dot(inverse[...], jnp.concatenate(columns, 1))
+        for part in range(parts):
+            for comp in range(2):
+                for target in range(4):
+                    lo = part * tile + comp * rows_j
+                    start = part * rows_j * outs + comp * 4 * group + target * group + focus
+                    spread[pl.ds(start, rows_j, stride=outs), :] = wave[
+                        lo:lo + rows_j, target * 128:target * 128 + 128
+                    ]
+        return carry
+
+    lax.fori_loop(0, group, transform, 0)
+
+    second = []
+    chip = me // 2
+    core = lax.rem(me, 2)
+    land = recv2.at[core, rows_of(chip, outs), :]
+
+    def pack_wave(part, carry):
+        for line in range(rows_j):
+            start = pl.multiple_of((part * rows_j + line) * outs, outs)
+            send2[part, :, line * 128:line * 128 + 128] = spread[pl.ds(start, outs), :].astype(
+                jnp.bfloat16
+            )
+        return carry
+
+    lax.fori_loop(0, parts, pack_wave, 0)
+    for step in STEPS:
+        peer = lax.rem(me + step, parts)
+        copy = pltpu.make_async_remote_copy(
+            src_ref=send2.at[peer],
+            dst_ref=land,
+            send_sem=sends2.at[step],
+            recv_sem=recvs2.at[step],
+            device_id=(freq, peer),
+            device_id_type=MESH,
+        )
+        copy.start()
+        second.append(copy)
+    own = pltpu.make_async_copy(send2.at[me], land, local_sem.at[1])
+    own.start()
+    own.wait()
+    for copy in second:
+        copy.wait()
+
+    nt = ((1,), (1,))
+    with_real = contract(recv2[0], panel[0, 0], nt) + contract(recv2[1], panel[0, 1], nt)
+    with_imag = contract(recv2[0], panel[1, 0], nt) + contract(recv2[1], panel[1, 1], nt)
+    half = outs // 2
+    pieces = []
+    for part in range(chips):
+        lo = part * outs
+        pieces.append(with_real[lo:lo + half] - with_imag[lo + half:lo + outs])
+        pieces.append(with_real[lo + half:lo + outs] + with_imag[lo:lo + half])
+    width = order.shape[0]
+    if width > chips * outs:
+        pieces.append(jnp.zeros((width - chips * outs, with_real.shape[1]), jnp.float32))
+    total[...] = jnp.concatenate(pieces, 0).T
+
+    sources = recv3.shape[1]
+    third = []
+    for step in STEPS:
+        peer = lax.rem(me + step, parts)
+        copy = pltpu.make_async_remote_copy(
+            src_ref=total.at[rows_of(peer, sources), :],
+            dst_ref=recv3.at[step],
+            send_sem=sends3.at[step],
+            recv_sem=recvs3.at[step],
+            device_id=(freq, peer),
+            device_id_type=MESH,
+        )
+        copy.start()
+        third.append(copy)
+    reflected = total[rows_of(me, sources), :]
+    for copy in third:
+        copy.wait()
+    for step in range(1, parts):
+        reflected = reflected + recv3[step]
+
+    weight = (freq + 1).astype(jnp.float32) * (2.0 / (freqs * (freqs + 1)))
+    squares = lax.dot_general(
+        jnp.ones((8, width), jnp.float32),
+        reflected * reflected * weight,
+        (nt, ((), ())),
+        precision=HIGHEST,
+        preferred_element_type=jnp.float32,
+    )
+    if sources < 128:
+        squares = jnp.concatenate([squares, jnp.zeros((8, 128 - sources), jnp.float32)], 1)
+    shared[0] = squares
+    fourth = []
+    for step in range(1, freqs):
+        copy = pltpu.make_async_remote_copy(
+            src_ref=shared.at[0],
+            dst_ref=shared.at[step],
+            send_sem=sends4.at[step],
+            recv_sem=recvs4.at[step],
+            device_id=(lax.rem(freq + step, freqs), me),
+            device_id_type=MESH,
+        )
+        copy.start()
+        fourth.append(copy)
+    placed = lax.dot_general(
+        reflected, order[...], (((1,), (0,)), ((), ())),
+        precision=HIGHEST, preferred_element_type=jnp.float32,
+    )
+    channels = 4 * foci
+    for comp in range(2):
+        lo = comp * (placed.shape[1] // 2)
+        focusing[:, comp, :] = direct[:, comp, :] - placed[:, lo:lo + channels]
+    for copy in fourth:
+        copy.wait()
+    summed = shared[0]
+    for step in range(1, freqs):
+        summed = summed + shared[step]
+    energy[...] = jnp.sqrt(summed[:, :sources] / (2 * channels) + 1e-06)
+
+
+STEPS = (4, 5, 3, 6, 2, 7, 1)
+
+
+def column_order(chips, group, width):
+    foci = chips * group
+    result = np.zeros((width, 2 * -(-4 * foci // 128) * 128), np.float32)
+    for chip in range(chips):
+        for comp in range(2):
+            for target in range(4):
+                for focus in range(group):
+                    here = ((chip * 2 + comp) * 4 + target) * group + focus
+                    there = comp * (result.shape[1] // 2) + target * foci + chip * group + focus
+                    result[here, there] = 1.0
+    return result
+
+
+def fused(field, live_count, line_owner, decomposer, reflection, direct_wave):
+    freqs = lax.axis_size("freq")
+    parts = lax.axis_size("line")
+    foci = field.shape[3]
+    rows_j = field.shape[4]
+    length = line_owner.shape[0]
+    chips = parts // 2
+    group = foci // chips
+    sources = direct_wave.shape[0]
+    all_sources = reflection.shape[1]
+    tile = 2 * rows_j
+    lanes = 4 * group * 128
+    outs = 8 * group
+    width = -(-chips * outs // 128) * 128
+
+    wavenum = jnp.arange(length, dtype=jnp.int32)
+    products = wavenum[:, None] * line_owner[None, :] % length
+    angles = products.astype(jnp.float32) * (2.0 * math.pi / length)
+    cosine, sine = jnp.cos(angles), jnp.sin(angles)
+    table = jnp.stack([jnp.stack([cosine, sine]), jnp.stack([-sine, cosine])])
+    table = table.reshape(2, 2, parts, rows_j, parts, rows_j)
+    table = table.transpose(2, 0, 3, 4, 1, 5).reshape(2 * length, 2 * length)
+    inverse = table.T / length
+    panel = reflection[0].reshape(all_sources, 2, rows_j, 2, 128).transpose(1, 3, 0, 2, 4)
+    panel = panel.reshape(2, 2, all_sources, rows_j * 128)
+    order = jnp.asarray(column_order(chips, group, width))
+
+    vmem = pl.BlockSpec(memory_space=pltpu.VMEM)
+    focusing, energy = pl.pallas_call(
+        lambda *refs: update_kernel(freqs, parts, foci, rows_j, *refs),
+        out_shape=(
+            jax.ShapeDtypeStruct(direct_wave.shape[:1] + direct_wave.shape[2:], jnp.float32),
+            jax.ShapeDtypeStruct((8, sources), jnp.float32),
+        ),
+        in_specs=[pl.BlockSpec(memory_space=pltpu.SMEM)] + [vmem] * 7,
+        out_specs=(vmem, vmem),
+        scratch_shapes=[
+            pltpu.VMEM((parts, tile, lanes + 2048), jnp.int16),
+            pltpu.VMEM((parts * tile, lanes + 2048), jnp.int16),
+            pltpu.VMEM((parts * tile, 2048), jnp.float32),
+            pltpu.VMEM((parts * rows_j * outs, 128), jnp.float32),
+            pltpu.VMEM((parts, outs, rows_j * 128), jnp.bfloat16),
+            pltpu.VMEM((2, chips * outs, rows_j * 128), jnp.bfloat16),
+            pltpu.VMEM((all_sources, width), jnp.float32),
+            pltpu.VMEM((parts, sources, width), jnp.float32),
+            pltpu.VMEM((freqs, 8, 128), jnp.float32),
+        ] + [pltpu.SemaphoreType.DMA((parts,))] * 6 + [pltpu.SemaphoreType.DMA((freqs,))] * 2
+        + [pltpu.SemaphoreType.DMA((2,))],
+        compiler_params=pltpu.CompilerParams(
+            collective_id=0, has_side_effects=True, vmem_limit_bytes=48 * 1024 * 1024
+        ),
+    )(
+        live_count, field[0], decomposer[0], table * (1.0 / FIELD_SCALE), inverse, panel,
+        direct_wave[:, 0], order,
+    )
+    return focusing[:, None], energy[0]
+
+
+def fits(field, line_owner, reflection, direct_wave):
+    parts = lax.axis_size("line")
+    rows_j = field.shape[4]
+    foci = field.shape[3]
+    return (
+        parts == 8
+        and rows_j == 8
+        and field.shape[0] == 1
+        and field.shape[5] == 256
+        and foci % (parts // 2) == 0
+        and (8 * foci // (parts // 2)) % 16 == 0
+        and line_owner.shape[0] == parts * rows_j
+        and direct_wave.shape[0] <= 128
+        and direct_wave.shape[0] % 8 == 0
+        and reflection.shape[1] <= 512
+    )
 
 
 def phase_tables(line_owner, length):
@@ -33,7 +378,7 @@
     return jnp.stack([jnp.stack(real_rows, 1), jnp.stack(imag_rows, 1)], 1)
 
 
-def on_device(field, live_count, line_owner, decomposer, reflection, direct_wave):
+def general(field, live_count, line_owner, decomposer, reflection, direct_wave):
     length = line_owner.shape[0]
     receivers = field.shape[5]
     cosine, sine_table = phase_tables(line_owner, length)
@@ -85,6 +430,14 @@
     return (focusing, trace_energy)
 
 
+def on_device(field, live_count, line_owner, decomposer, reflection, direct_wave):
+    if fits(field, line_owner, reflection, direct_wave):
+        body = fused
+    else:
+        body = general
+    return body(field, live_count, line_owner, decomposer, reflection, direct_wave)
+
+
 def solution(mesh):
     return jax.shard_map(
         on_device,

time: 181 us -> 83.7 us (0.46)
  waiting for transfers between devices: 108 us -> 0 us
  Pallas kernels: 0 us -> 65.7 us
  blocking collectives: 33.2 us -> 0 us
  between operations: 14.9 us -> 0.73 us
  local copies, waits for them, and re-layouts: 7.24 us -> 15.6 us
  starting transfers between devices: 6.53 us -> 0 us
  other arithmetic: 7.31 us -> 1.4 us
  matrix products: 4.03 us -> 0 us
    pallas_call x0 -> x1, Pallas kernels: none -> 65.7 us  [fused(): pl.pallas_call(lambda *refs: update_kernel(freqs, parts, foci, rows_j, *r...]
    all_to_all x1 -> x0, waiting for transfers between devices: 54.3 us -> none  [on_device(): lax.all_to_all(live_field, 'line', split_axis=3, concat_axis=4, tiled=True)]
    unnamed x3 -> x0, waiting for transfers between devices: 53.5 us -> none
    all_to_all x1 -> x0, blocking collectives: 23.4 us -> none  [on_device(): lax.all_to_all(space_all.astype(jnp.bfloat16), 'line', split_axis=4, conc...]
    psum x1 -> x0, blocking collectives: 9.81 us -> none  [on_device(): energy_sum = lax.psum(partial_value, 'freq')]
    all_to_all x1 -> x0, starting transfers between devices: 6.46 us -> none  [on_device(): lax.all_to_all(live_field, 'line', split_axis=3, concat_axis=4, tiled=True)]
    another operation x1 -> x2, local copies, waits for them, and re-layouts: 0.36 us -> 4.78 us  [fused(): reflection[0].reshape(all_sources, 2, rows_j, 2, 128)]
    dot_general x3 -> x0, matrix products: 4.03 us -> none  [the longest x1 1.57 us: on_device(): jnp.einsum('yxkj,fxiojr->fyiokr', forward_table, every_line, precision=la...]
  transfers between devices with their start and end apart: 3 -> 0, of which waited for: 2 -> 0; matrix products, arithmetic and copies ran while one was open for 3% -> 0% of each run, Pallas kernels for 0% -> 0%
where the time goes in v1:
time: 83.7 us; the launch traced here: 83.5 us
  Pallas kernels  65.7 us (78%)
  local copies, waits for them, and re-layouts  15.6 us (19%)
  other arithmetic  1.4 us (2%)
    pallas_call x1, Pallas kernels, fused(): pl.pallas_call(lambda *refs: update_kernel(freqs, parts, foci, rows_j, *r...  65.7 us
    another operation x2, local copies, waits for them, and re-layouts, fused(): reflection[0].reshape(all_sources, 2, rows_j, 2, 128)  4.78 us
    reshape x1, local copies, waits for them, and re-layouts, fused(): panel = panel.reshape(2, 2, all_sources, rows_j * 128)  2.88 us
    div x2, local copies, waits for them, and re-layouts, fused(): inverse = table.T / length  2.44 us
    mul x2, local copies, waits for them, and re-layouts, fused(): table * (1.0 / FIELD_SCALE)  2.27 us
    unnamed x11, local copies, waits for them, and re-layouts  2.03 us

profile of v1, /device:TPU:0, one launch (start us, length us, event | category | flops | bytes accessed | tf_op | source)
XLA Modules:
  0.0 83.5 jit_solution(269804185727326720)
XLA Ops:
  0.6 0.7 mul.85
  1.4 1.1 %fusion.3 = (f32[1,1,8,8,8,8]{5,4,3,2,1,0:T(8,128)S(1)}, f32[1,1,8,8,8,8]{5,4,3,2,1,0:T(8,128)S(1)}, f32[1,1,8,8,8,8]{5,4,3,2,1,0:T(8,128)S(1)}) fusion(s32[8,8]{1,0:T(8,128)S(1)} %mul.85, s32[8,8]{1,0:T(8,128)S(1)} %multiply_add_fusion), kind=kLoop, calls=%fused_computation.12 | loop fusion | flops 61440 | bytes 49664 | tf_op jit(solution)/shard_map/sin | solution.py:296
  2.5 0.3 multiply_bitcast_fusion
  2.8 1.0 %copy.13 = f32[8,2,8,8,2,8]{2,1,0,5,4,3:T(2,128)S(1)} copy(f32[8,2,8,8,2,8]{5,3,2,0,4,1:T(8,128)S(1)} %get-tuple-element.10) | data formatting | bytes 131072 | tf_op jit(solution)/shard_map/div | solution.py:300
  3.8 1.5 %div.15 = f32[128,128]{0,1:T(8,128)S(1)} reshape(f32[8,2,8,8,2,8]{2,1,0,5,4,3:T(2,128)S(1)} %copy.13) | data formatting | bytes 131072 | tf_op jit(solution)/shard_map/div | solution.py:300
  5.2 0.8 copy.12
  6.0 1.5 %mul.93.refs_3_ = f32[128,128]{1,0:T(8,128)S(1)} reshape(f32[8,2,8,8,2,8]{5,4,3,2,1,0:T(2,128)S(1)} %copy.12) | data formatting | bytes 131072 | tf_op jit(solution)/shard_map/mul | solution.py:330
  7.5 3.2 %reshape_squeeze.3 = bf16[256,2,8,2,128]{4,3,2,1,0:T(2,128)(2,1)S(1)} reshape(bf16[1,256,2,2048]{3,2,1,0:T(2,128)(2,1)} %param.11) | data formatting | bytes 4194304 | tf_op jit(solution)/shard_map/reshape;squeeze | solution.py:301
  10.7 1.6 %copy.17 = bf16[256,2,8,2,128]{4,2,0,3,1:T(8,128)(2,1)} copy(bf16[256,2,8,2,128]{4,3,2,1,0:T(2,128)(2,1)S(1)} %reshape_squeeze.3) | data formatting | bytes 4194304 | tf_op jit(solution)/shard_map/reshape;squeeze | solution.py:301
  12.3 0.0 copy-start.1
  12.3 0.0 copy-start.2
  12.3 0.0 copy-start.3
  12.3 0.0 copy-start.4
  12.3 2.9 %reshape.138.refs_5_ = bf16[2,2,256,1024]{3,2,1,0:T(8,128)(2,1)S(1)} reshape(bf16[2,2,256,8,128]{4,3,2,1,0:T(8,128)(2,1)} %bitcast.25) | data formatting | bytes 4194304 | tf_op jit(solution)/shard_map/reshape | solution.py:302
  15.2 0.0 copy-done.1
  15.2 0.0 copy-done.2
  15.2 0.0 copy-done.3
  15.2 0.0 copy-done.4
  15.2 0.0 copy-start
  15.2 1.4 %copy-done = f32[1,2,4,24,8,256]{5,4,3,2,1,0:T(8,128)S(1)} copy-done((f32[1,2,4,24,8,256]{5,4,3,2,1,0:T(8,128)S(1)}, f32[1,2,4,24,8,256]{5,4,3,2,1,0:T(8,128)}, u32[]{:S(2)}) %copy-start) | copy-done | bytes 1572888
  16.6 65.7 %shard_map.86 = (f32[32,2,96]{2,1,0:T(2,128)S(1)}, f32[8,32]{1,0:T(8,128)S(1)}) custom-call(s32[8]{0:T(128)S(1)} %copy-done.4, f32[2,4,24,8,256]{4,3,2,1,0:T(8,128)S(1)} %bitcast.20, f32[2,4,4,8,256]{4,3,2,1,0:T(8,128)S(1)} %bitcast.22, f32[128,128]{1,0:T(8,128)S(1)} %mul.93.refs_3_, f32[128,128]{1,0:T(8,128)S(1)} %bitcast.21, ...), custom_call_target="tpu_custom_call" | custom-call | tf_op jit(solution)/shard_map/pallas_call | solution.py:306
  82.3 0.5 slice_bitcast_fusion
  82.9 0.6 copy.19
  (1 shorter events, 0.0 us)
Async XLA Ops:
  12.3 2.9 %copy-start.1 = (f32[1,2,4,4,8,256]{5,4,3,2,1,0:T(8,128)S(1)}, f32[1,2,4,4,8,256]{5,4,3,2,1,0:T(8,128)}, u32[]{:S(2)}) copy-start(f32[1,2,4,4,8,256]{5,4,3,2,1,0:T(8,128)} %param.10) | copy-start | bytes 786436
  12.3 2.9 %copy-start.2 = (f32[256,256]{1,0:T(8,128)S(1)}, f32[256,256]{1,0:T(8,128)}, u32[]{:S(2)}) copy-start(f32[256,256]{1,0:T(8,128)} %constant.29.clone.refs_7_) | copy-start | bytes 786436
  12.3 2.9 %copy-start.3 = (f32[32,1,2,96]{3,2,1,0:T(2,128)S(1)}, f32[32,1,2,96]{3,2,1,0:T(2,128)}, u32[]{:S(2)}) copy-start(f32[32,1,2,96]{3,2,1,0:T(2,128)} %param.12) | copy-start | bytes 73732
  12.3 2.9 %copy-start.4 = (s32[8]{0:T(128)S(1)}, s32[8]{0:T(128)}, u32[]{:S(2)}) copy-start(s32[8]{0:T(128)} %refs_0_.1) | copy-start | bytes 100
  15.2 1.4 %copy-start = (f32[1,2,4,24,8,256]{5,4,3,2,1,0:T(8,128)S(1)}, f32[1,2,4,24,8,256]{5,4,3,2,1,0:T(8,128)}, u32[]{:S(2)}) copy-start(f32[1,2,4,24,8,256]{5,4,3,2,1,0:T(8,128)} %param.7) | copy-start | bytes 4718596

commit v2 on v0

--- a/solution.py
+++ b/solution.py
@@ -2,8 +2,401 @@
 
 import jax
 import jax.numpy as jnp
+import numpy as np
 from jax import lax
+from jax.experimental import pallas as pl
+from jax.experimental.pallas import tpu as pltpu
 from jax.sharding import PartitionSpec as P
+
+MESH = pl.DeviceIdType.MESH
+HIGHEST = lax.Precision.HIGHEST
+FIELD_SCALE = 5400.0
+OPERATOR_SCALE = 13600.0
+
+
+def contract(left, right, dims):
+    return lax.dot_general(left, right, (dims, ((), ())), preferred_element_type=jnp.float32)
+
+
+def split(value):
+    high = value.astype(jnp.bfloat16)
+    return high, (value - high.astype(jnp.float32)).astype(jnp.bfloat16)
+
+
+def fine_dot(left, right):
+    left_high, left_low = split(left)
+    right_high, right_low = split(right)
+    dims = ((1,), (0,))
+    return contract(left_high, right_high, dims) + (
+        contract(left_high, right_low, dims) + contract(left_low, right_high, dims)
+    )
+
+
+def coded(value, scale):
+    return jnp.round(value * scale).astype(jnp.int32).astype(jnp.int16)
+
+
+def update_kernel(
+    freqs, parts, foci, rows_j,
+    counts, owner, field_hbm, operator, panel_hbm, direct, order,
+    focusing, energy,
+    field, send_op, recv_op, weights, send1, recv1, tables, raw, panel, spread, send2, recv2,
+    total, recv3, shared,
+    sends0, recvs0, sends1, recvs1, sends2, recvs2, sends3, recvs3, sends4, recvs4, local_sem,
+):
+    chips = parts // 2
+    group = foci // chips
+    chunks = group // 2
+    tile = 2 * rows_j
+    length = parts * rows_j
+    me = lax.axis_index("line")
+    freq = lax.axis_index("freq")
+    chip, core = me // 2, lax.rem(me, 2)
+    peers = []
+    for other in (lax.rem(chip + 2, 4), 3 - chip, chip + 1 - 2 * lax.rem(chip, 2)):
+        peers.append((other, core))
+        peers.append((other, 1 - core))
+    peers.append((chip, 1 - core))
+
+    loads = []
+    for chunk in range(chunks):
+        loads.append(
+            pltpu.make_async_copy(field_hbm.at[:, :, :, chunk], field.at[chunk], local_sem.at[chunk])
+        )
+        loads[-1].start()
+    panel_load = pltpu.make_async_copy(panel_hbm, raw, local_sem.at[chunks])
+    panel_load.start()
+
+    barrier = pltpu.get_barrier_semaphore()
+    for other, side in peers:
+        pl.semaphore_signal(
+            barrier, inc=1, device_id=(freq, other * 2 + side), device_id_type=MESH
+        )
+    for step in range(1, freqs):
+        pl.semaphore_signal(
+            barrier, inc=1, device_id=(lax.rem(freq + step, freqs), me), device_id_type=MESH
+        )
+
+    row = lax.broadcasted_iota(jnp.int32, (rows_j, 256), 0)
+    count = jnp.zeros((rows_j, 256), jnp.int32)
+    for line in range(rows_j):
+        count = jnp.where(row == line, counts[line], count)
+    live = lax.broadcasted_iota(jnp.int32, (rows_j, 256), 1) < count
+
+    def rows_of(part, size):
+        return pl.ds(pl.multiple_of(part * size, size), size)
+
+    mine = rows_of(me, tile)
+
+    def send(source, target, number, sends, recvs):
+        other, side = peers[number]
+        copy = pltpu.make_async_remote_copy(
+            src_ref=source,
+            dst_ref=target,
+            send_sem=sends.at[number],
+            recv_sem=recvs.at[number],
+            device_id=(freq, other * 2 + side),
+            device_id_type=MESH,
+        )
+        copy.start()
+        return copy
+
+    def pack_operator(target, carry):
+        for source in range(4):
+            block = coded(operator[:, target, source], OPERATOR_SCALE).reshape(tile, 256)
+            at = pl.ds(pl.multiple_of((target * 4 + source) * 128, 128), 128)
+            send_op[0, :, at] = block[:, :128]
+            send_op[1, :, at] = block[:, 128:]
+        return carry
+
+    lax.fori_loop(0, 4, pack_operator, 0)
+    pl.semaphore_wait(barrier, parts - 1 + freqs - 1)
+    zeroth = [
+        send(send_op.at[side], recv_op.at[mine, :], number, sends0, recvs0)
+        for number, (other, side) in enumerate(peers)
+    ]
+    recv_op[mine, :] = send_op[core]
+
+    first = []
+    for chunk in range(chunks):
+        loads[chunk].wait()
+
+        def pack_field(to, carry):
+            for focus in range(2):
+                for source in range(4):
+                    value = jnp.where(live[None], field[chunk, :, source, to, focus], 0.0)
+                    block = coded(value, FIELD_SCALE).reshape(tile, 256)
+                    lo = (focus * 4 + source) * 128
+                    send1[chunk, 2 * to, :, lo:lo + 128] = block[:, :128]
+                    send1[chunk, 2 * to + 1, :, lo:lo + 128] = block[:, 128:]
+            return carry
+
+        lax.fori_loop(0, chips, pack_field, 0)
+        first.append([
+            send(send1.at[chunk, other * 2 + side], recv1.at[chunk, mine, :], number,
+                 sends1.at[chunk], recvs1.at[chunk])
+            for number, (other, side) in enumerate(peers)
+        ])
+        recv1[chunk, mine, :] = send1[chunk, me]
+
+    column = lax.broadcasted_iota(jnp.int32, (length, 2 * length), 1)
+    line = column // tile * rows_j + lax.rem(column, rows_j)
+    pick = line == lax.broadcasted_iota(jnp.int32, (length, 2 * length), 0)
+    owners = contract(
+        jnp.broadcast_to(owner[...].astype(jnp.float32).astype(jnp.bfloat16), (8, length)),
+        pick.astype(jnp.float32).astype(jnp.bfloat16),
+        ((1,), (0,)),
+    )[:1].astype(jnp.int32)
+    across = lax.broadcasted_iota(jnp.int32, (2 * length, 2 * length), 1)
+    down = lax.broadcasted_iota(jnp.int32, (2 * length, 2 * length), 0)
+    wavenum = down // tile * rows_j + lax.rem(down, rows_j)
+    quarter = lax.rem(down, tile) // rows_j - lax.rem(across, tile) // rows_j
+    turns = lax.rem(wavenum * owners + (quarter + 4) * (length // 4), length)
+    wheel = jnp.cos(turns.astype(jnp.float32) * (2.0 * math.pi / length))
+    tables[0] = wheel * (1.0 / FIELD_SCALE)
+    tables[1] = wheel.T * (1.0 / length)
+
+    panel_load.wait()
+    all_sources = raw.shape[0]
+
+    def unpack_panel(block, carry):
+        at = pl.ds(pl.multiple_of(block * 16, 16), 16)
+        values = raw[at].astype(jnp.float32)
+        for comp in range(2):
+            half = values[:, comp, :].astype(jnp.bfloat16)
+            for line in range(rows_j):
+                for side in range(2):
+                    lo = (line * 2 + side) * 128
+                    panel[comp, side, at, line * 128:line * 128 + 128] = half[:, lo:lo + 128]
+        return carry
+
+    lax.fori_loop(0, all_sources // 16, unpack_panel, 0)
+
+    for copy in zeroth:
+        copy.wait()
+    for block in range(16):
+        lo = block * 128
+        weights[:, lo:lo + 128] = recv_op[:, lo:lo + 128].astype(jnp.float32) * (
+            1.0 / OPERATOR_SCALE
+        )
+
+    second = []
+    land_rows = rows_of(chip, 16)
+    for chunk in range(chunks):
+        for copy in first[chunk]:
+            copy.wait()
+
+        def transform(focus, carry):
+            at = pl.ds(pl.multiple_of(focus * 512, 512), 512)
+            values = recv1[chunk, :, at].astype(jnp.float32)
+            spectrum = fine_dot(tables[0], values).reshape(parts, 2, rows_j, 512)
+            real, imag = spectrum[:, 0], spectrum[:, 1]
+            columns = []
+            for target in range(4):
+                out_real, out_imag = None, None
+                for source in range(4):
+                    lo = (target * 4 + source) * 128
+                    weight = weights[:, lo:lo + 128].reshape(parts, 2, rows_j, 128)
+                    wr, wi = weight[:, 0], weight[:, 1]
+                    fr = real[:, :, source * 128:source * 128 + 128]
+                    fi = imag[:, :, source * 128:source * 128 + 128]
+                    tr = wr * fr - wi * fi
+                    ti = wr * fi + wi * fr
+                    out_real = tr if out_real is None else out_real + tr
+                    out_imag = ti if out_imag is None else out_imag + ti
+                columns.append(jnp.stack([out_real, out_imag], 1).reshape(2 * length, 128))
+            wave = fine_dot(tables[1], jnp.concatenate(columns, 1))
+            for part in range(parts):
+                for comp in range(2):
+                    for target in range(4):
+                        lo = part * tile + comp * rows_j
+                        start = part * rows_j * 16 + comp * 8 + target * 2 + focus
+                        spread[pl.ds(start, rows_j, stride=16), :] = wave[
+                            lo:lo + rows_j, target * 128:target * 128 + 128
+                        ]
+            return carry
+
+        lax.fori_loop(0, 2, transform, 0)
+
+        def pack_wave(part, carry):
+            for line in range(rows_j):
+                start = pl.multiple_of((part * rows_j + line) * 16, 16)
+                send2[chunk, part, :, line * 128:line * 128 + 128] = spread[
+                    pl.ds(start, 16), :
+                ].astype(jnp.bfloat16)
+            return carry
+
+        lax.fori_loop(0, parts, pack_wave, 0)
+        second.append([
+            send(send2.at[chunk, other * 2 + side], recv2.at[chunk, core, land_rows, :], number,
+                 sends2.at[chunk], recvs2.at[chunk])
+            for number, (other, side) in enumerate(peers)
+        ])
+        recv2[chunk, core, land_rows, :] = send2[chunk, me]
+
+    nt = ((1,), (1,))
+    pieces = []
+    for chunk in range(chunks):
+        for copy in second[chunk]:
+            copy.wait()
+        wave0, wave1 = recv2[chunk, 0], recv2[chunk, 1]
+        with_real = contract(wave0, panel[0, 0], nt) + contract(wave1, panel[0, 1], nt)
+        with_imag = contract(wave0, panel[1, 0], nt) + contract(wave1, panel[1, 1], nt)
+        for part in range(chips):
+            lo = part * 16
+            pieces.append(with_real[lo:lo + 8] - with_imag[lo + 8:lo + 16])
+            pieces.append(with_real[lo + 8:lo + 16] + with_imag[lo:lo + 8])
+    width = order.shape[0]
+    if width > 8 * foci:
+        pieces.append(jnp.zeros((width - 8 * foci, all_sources), jnp.float32))
+    total[...] = jnp.concatenate(pieces, 0).T
+
+    sources = recv3.shape[1]
+    third = [
+        send(total.at[rows_of(other * 2 + side, sources), :], recv3.at[number], number,
+             sends3, recvs3)
+        for number, (other, side) in enumerate(peers)
+    ]
+    reflected = total[rows_of(me, sources), :]
+    for number, copy in enumerate(third):
+        copy.wait()
+    for number in range(parts - 1):
+        reflected = reflected + recv3[number]
+
+    weight = (freq + 1).astype(jnp.float32) * (2.0 / (freqs * (freqs + 1)))
+    squares = lax.dot_general(
+        jnp.ones((8, width), jnp.float32),
+        reflected * reflected * weight,
+        (nt, ((), ())),
+        precision=HIGHEST,
+        preferred_element_type=jnp.float32,
+    )
+    if sources < 128:
+        squares = jnp.concatenate([squares, jnp.zeros((8, 128 - sources), jnp.float32)], 1)
+    shared[0] = squares
+    fourth = []
+    for step in range(1, freqs):
+        copy = pltpu.make_async_remote_copy(
+            src_ref=shared.at[0],
+            dst_ref=shared.at[step],
+            send_sem=sends4.at[step],
+            recv_sem=recvs4.at[step],
+            device_id=(lax.rem(freq + step, freqs), me),
+            device_id_type=MESH,
+        )
+        copy.start()
+        fourth.append(copy)
+    placed = lax.dot_general(
+        reflected, order[...], (((1,), (0,)), ((), ())),
+        precision=HIGHEST, preferred_element_type=jnp.float32,
+    )
+    channels = 4 * foci
+    for comp in range(2):
+        lo = comp * (placed.shape[1] // 2)
+        focusing[:, comp, :] = direct[:, comp, :] - placed[:, lo:lo + channels]
+    for copy in fourth:
+        copy.wait()
+    summed = shared[0]
+    for step in range(1, freqs):
+        summed = summed + shared[step]
+    energy[...] = jnp.sqrt(summed[:1, :sources] / (2 * channels) + 1e-06)
+
+
+def column_order(chips, group, width):
+    foci = chips * group
+    result = np.zeros((width, 2 * -(-4 * foci // 128) * 128), np.float32)
+    here = 0
+    for chunk in range(group // 2):
+        for chip in range(chips):
+            for comp in range(2):
+                for target in range(4):
+                    for focus in range(2):
+                        at = target * foci + chip * group + chunk * 2 + focus
+                        result[here, comp * (result.shape[1] // 2) + at] = 1.0
+                        here += 1
+    return result
+
+
+def fused(field, live_count, line_owner, decomposer, reflection, direct_wave):
+    freqs = lax.axis_size("freq")
+    parts = lax.axis_size("line")
+    foci = field.shape[3]
+    rows_j = field.shape[4]
+    length = line_owner.shape[0]
+    chips = parts // 2
+    group = foci // chips
+    chunks = group // 2
+    sources = direct_wave.shape[0]
+    all_sources = reflection.shape[1]
+    tile = 2 * rows_j
+    width = -(-8 * foci // 128) * 128
+    order = jnp.asarray(column_order(chips, group, width))
+
+    vmem = pl.BlockSpec(memory_space=pltpu.VMEM)
+    smem = pl.BlockSpec(memory_space=pltpu.SMEM)
+    far = pl.BlockSpec(memory_space=pl.ANY)
+    pair = pltpu.SemaphoreType.DMA((parts - 1,))
+    many = pltpu.SemaphoreType.DMA((chunks, parts - 1))
+    focusing, energy = pl.pallas_call(
+        lambda *refs: update_kernel(freqs, parts, foci, rows_j, *refs),
+        out_shape=(
+            jax.ShapeDtypeStruct(direct_wave.shape[:1] + direct_wave.shape[2:], jnp.float32),
+            jax.ShapeDtypeStruct((1, sources), jnp.float32),
+        ),
+        in_specs=[smem, vmem, far, vmem, far, vmem, vmem],
+        out_specs=(vmem, vmem),
+        scratch_shapes=[
+            pltpu.VMEM((chunks, 2, 4, chips, 2, rows_j, 256), jnp.float32),
+            pltpu.VMEM((2, tile, 2048), jnp.int16),
+            pltpu.VMEM((parts * tile, 2048), jnp.int16),
+            pltpu.VMEM((parts * tile, 2048), jnp.float32),
+            pltpu.VMEM((chunks, parts, tile, 1024), jnp.int16),
+            pltpu.VMEM((chunks, parts * tile, 1024), jnp.int16),
+            pltpu.VMEM((2, 2 * length, 2 * length), jnp.float32),
+            pltpu.VMEM(reflection.shape[1:], jnp.bfloat16),
+            pltpu.VMEM((2, 2, all_sources, rows_j * 128), jnp.bfloat16),
+            pltpu.VMEM((parts * rows_j * 16, 128), jnp.float32),
+            pltpu.VMEM((chunks, parts, 16, rows_j * 128), jnp.bfloat16),
+            pltpu.VMEM((chunks, 2, chips * 16, rows_j * 128), jnp.bfloat16),
+            pltpu.VMEM((all_sources, width), jnp.float32),
+            pltpu.VMEM((parts - 1, sources, width), jnp.float32),
+            pltpu.VMEM((freqs, 8, 128), jnp.float32),
+            pair, pair, many, many, many, many, pair, pair,
+            pltpu.SemaphoreType.DMA((freqs,)),
+            pltpu.SemaphoreType.DMA((freqs,)),
+            pltpu.SemaphoreType.DMA((chunks + 1,)),
+        ],
+        compiler_params=pltpu.CompilerParams(
+            collective_id=0, has_side_effects=True, vmem_limit_bytes=48 * 1024 * 1024
+        ),
+    )(
+        live_count,
+        line_owner[None],
+        field.reshape(2, 4, chips, chunks, 2, rows_j, 256),
+        decomposer[0],
+        reflection[0],
+        direct_wave[:, 0],
+        order,
+    )
+    return focusing[:, None], energy[0]
+
+
+def fits(field, line_owner, reflection, direct_wave):
+    parts = lax.axis_size("line")
+    rows_j = field.shape[4]
+    foci = field.shape[3]
+    return (
+        parts == 8
+        and rows_j == 8
+        and field.shape[0] == 1
+        and field.shape[5] == 256
+        and foci % parts == 0
+        and line_owner.shape[0] == parts * rows_j
+        and direct_wave.shape[0] <= 128
+        and direct_wave.shape[0] % 8 == 0
+        and reflection.shape[1] % 256 == 0
+        and reflection.shape[1] <= 512
+    )
 
 
 def phase_tables(line_owner, length):
@@ -33,7 +426,7 @@
     return jnp.stack([jnp.stack(real_rows, 1), jnp.stack(imag_rows, 1)], 1)
 
 
-def on_device(field, live_count, line_owner, decomposer, reflection, direct_wave):
+def general(field, live_count, line_owner, decomposer, reflection, direct_wave):
     length = line_owner.shape[0]
     receivers = field.shape[5]
     cosine, sine_table = phase_tables(line_owner, length)
@@ -85,6 +478,14 @@
     return (focusing, trace_energy)
 
 
+def on_device(field, live_count, line_owner, decomposer, reflection, direct_wave):
+    if fits(field, line_owner, reflection, direct_wave):
+        body = fused
+    else:
+        body = general
+    return body(field, live_count, line_owner, decomposer, reflection, direct_wave)
+
+
 def solution(mesh):
     return jax.shard_map(
         on_device,

time: 181 us -> 73.9 us (0.41)
  waiting for transfers between devices: 108 us -> 0 us
  Pallas kernels: 0 us -> 64.9 us
  blocking collectives: 33.2 us -> 0 us
  between operations: 14.9 us -> 0.65 us
  other arithmetic: 7.31 us -> 0 us
  starting transfers between devices: 6.53 us -> 0 us
  matrix products: 4.03 us -> 0 us
    pallas_call x0 -> x1, Pallas kernels: none -> 64.9 us  [fused(): pl.pallas_call(lambda *refs: update_kernel(freqs, parts, foci, rows_j, *r...]
    all_to_all x1 -> x0, waiting for transfers between devices: 54.3 us -> none  [on_device(): lax.all_to_all(live_field, 'line', split_axis=3, concat_axis=4, tiled=True)]
    unnamed x3 -> x0, waiting for transfers between devices: 53.5 us -> none
    all_to_all x1 -> x0, blocking collectives: 23.4 us -> none  [on_device(): lax.all_to_all(space_all.astype(jnp.bfloat16), 'line', split_axis=4, conc...]
    psum x1 -> x0, blocking collectives: 9.81 us -> none  [on_device(): energy_sum = lax.psum(partial_value, 'freq')]
    all_to_all x1 -> x0, starting transfers between devices: 6.46 us -> none  [on_device(): lax.all_to_all(live_field, 'line', split_axis=3, concat_axis=4, tiled=True)]
    unnamed x9 -> x16, local copies, waits for them, and re-layouts: 2.04 us -> 8.09 us
    dot_general x3 -> x0, matrix products: 4.03 us -> none  [the longest x1 1.57 us: on_device(): jnp.einsum('yxkj,fxiojr->fyiokr', forward_table, every_line, precision=la...]
  transfers between devices with their start and end apart: 3 -> 0, of which waited for: 2 -> 0; matrix products, arithmetic and copies ran while one was open for 3% -> 0% of each run, Pallas kernels for 0% -> 0%
where the time goes in v2:
time: 73.9 us; the launch traced here: 73.6 us
  Pallas kernels  64.9 us (88%)
  local copies, waits for them, and re-layouts  8.09 us (11%)
    pallas_call x1, Pallas kernels, fused(): pl.pallas_call(lambda *refs: update_kernel(freqs, parts, foci, rows_j, *r...  64.9 us
    unnamed x16, local copies, waits for them, and re-layouts  8.09 us

profile of v2, /device:TPU:0, one launch (start us, length us, event | category | flops | bytes accessed | tf_op | source)
XLA Modules:
  0.0 73.6 jit_solution(11086126348170157431)
XLA Ops:
  0.6 0.0 copy-start
  0.6 1.6 %copy-done = bf16[1,256,2,2048]{3,2,1,0:T(2,128)(2,1)S(1)} copy-done((bf16[1,256,2,2048]{3,2,1,0:T(2,128)(2,1)S(1)}, bf16[1,256,2,2048]{3,2,1,0:T(2,128)(2,1)}, u32[]{:S(2)}) %copy-start) | copy-done | bytes 2097176
  2.2 0.0 copy-start.1
  2.2 1.4 %copy-done.1 = f32[1,2,4,24,8,256]{5,4,3,2,1,0:T(8,128)S(1)} copy-done((f32[1,2,4,24,8,256]{5,4,3,2,1,0:T(8,128)S(1)}, f32[1,2,4,24,8,256]{5,4,3,2,1,0:T(8,128)}, u32[]{:S(2)}) %copy-start.1) | copy-done | bytes 1572888
  3.6 0.0 copy-start.2
  3.6 0.9 %copy-done.2 = f32[1,2,4,4,8,256]{5,4,3,2,1,0:T(8,128)S(1)} copy-done((f32[1,2,4,4,8,256]{5,4,3,2,1,0:T(8,128)S(1)}, f32[1,2,4,4,8,256]{5,4,3,2,1,0:T(8,128)}, u32[]{:S(2)}) %copy-start.2) | copy-done | bytes 262168
  4.6 0.0 copy-start.3
  4.6 0.9 %copy-done.3 = f32[256,256]{1,0:T(8,128)S(1)} copy-done((f32[256,256]{1,0:T(8,128)S(1)}, f32[256,256]{1,0:T(8,128)}, u32[]{:S(2)}) %copy-start.3) | copy-done | bytes 262168
  5.5 0.0 copy-start.4
  5.5 0.8 %copy-done.4 = f32[32,1,2,96]{3,2,1,0:T(2,128)S(1)} copy-done((f32[32,1,2,96]{3,2,1,0:T(2,128)S(1)}, f32[32,1,2,96]{3,2,1,0:T(2,128)}, u32[]{:S(2)}) %copy-start.4) | copy-done | bytes 24600
  6.3 0.0 copy-start.5
  6.3 0.7 copy-done.5
  6.9 0.0 copy-start.6
  6.9 0.7 copy-done.6
  7.6 64.9 %shard_map.86 = (f32[32,2,96]{2,1,0:T(2,128)S(1)}, f32[1,32]{1,0:T(1,128)S(1)}) custom-call(s32[8]{0:T(128)S(1)} %copy-done.5, s32[1,64]{1,0:T(1,128)S(1)} %bitcast.14, f32[2,4,4,3,2,8,256]{6,5,4,3,2,1,0:T(8,128)S(1)} %bitcast.10, f32[2,4,4,8,256]{4,3,2,1,0:T(8,128)S(1)} %bitcast.11, bf16[256,2,2048]{2,1,0:T(2,128)(2,1)S(1)} %bitcast.9, ...), custom_call_target="tpu_custom_call" | custom-call | tf_op jit(solution)/shard_map/pallas_call | solution.py:340
  72.5 0.6 copy.12
  73.1 0.5 copy.13
Async XLA Ops:
  0.6 1.6 %copy-start = (bf16[1,256,2,2048]{3,2,1,0:T(2,128)(2,1)S(1)}, bf16[1,256,2,2048]{3,2,1,0:T(2,128)(2,1)}, u32[]{:S(2)}) copy-start(bf16[1,256,2,2048]{3,2,1,0:T(2,128)(2,1)} %param.11) | copy-start | bytes 6291460
  2.2 1.4 %copy-start.1 = (f32[1,2,4,24,8,256]{5,4,3,2,1,0:T(8,128)S(1)}, f32[1,2,4,24,8,256]{5,4,3,2,1,0:T(8,128)}, u32[]{:S(2)}) copy-start(f32[1,2,4,24,8,256]{5,4,3,2,1,0:T(8,128)} %param.7) | copy-start | bytes 4718596
  3.6 0.9 %copy-start.2 = (f32[1,2,4,4,8,256]{5,4,3,2,1,0:T(8,128)S(1)}, f32[1,2,4,4,8,256]{5,4,3,2,1,0:T(8,128)}, u32[]{:S(2)}) copy-start(f32[1,2,4,4,8,256]{5,4,3,2,1,0:T(8,128)} %param.10) | copy-start | bytes 786436
  4.6 0.9 %copy-start.3 = (f32[256,256]{1,0:T(8,128)S(1)}, f32[256,256]{1,0:T(8,128)}, u32[]{:S(2)}) copy-start(f32[256,256]{1,0:T(8,128)} %constant.2.clone.refs_6_) | copy-start | bytes 786436
  5.5 0.8 %copy-start.4 = (f32[32,1,2,96]{3,2,1,0:T(2,128)S(1)}, f32[32,1,2,96]{3,2,1,0:T(2,128)}, u32[]{:S(2)}) copy-start(f32[32,1,2,96]{3,2,1,0:T(2,128)} %param.12) | copy-start | bytes 73732
  6.3 0.7 copy-start.5
  6.9 0.7 copy-start.6

commit v3 on v2

--- a/solution.py
+++ b/solution.py
@@ -41,7 +41,7 @@
     counts, owner, field_hbm, operator, panel_hbm, direct, order,
     focusing, energy,
     field, send_op, recv_op, weights, send1, recv1, tables, raw, panel, spread, send2, recv2,
-    total, recv3, shared,
+    total, twin, joined, recv3, shared,
     sends0, recvs0, sends1, recvs1, sends2, recvs2, sends3, recvs3, sends4, recvs4, local_sem,
 ):
     chips = parts // 2
@@ -114,8 +114,24 @@
     zeroth = [
         send(send_op.at[side], recv_op.at[mine, :], number, sends0, recvs0)
         for number, (other, side) in enumerate(peers)
+        if number >= 4
     ]
     recv_op[mine, :] = send_op[core]
+    half_rows = parts * tile // 2
+    near = rows_of(chip // 2, half_rows)
+    away = rows_of(1 - chip // 2, half_rows)
+    inner = jnp.logical_or(chip == 1, chip == 2)
+
+    def relay(rows, number, slot):
+        other, side = peers[number]
+        return pltpu.make_async_remote_copy(
+            src_ref=recv_op.at[rows, :],
+            dst_ref=recv_op.at[rows, :],
+            send_sem=sends0.at[slot],
+            recv_sem=recvs0.at[slot],
+            device_id=(freq, other * 2 + side),
+            device_id_type=MESH,
+        )
 
     first = []
     for chunk in range(chunks):
@@ -138,6 +154,18 @@
             for number, (other, side) in enumerate(peers)
         ])
         recv1[chunk, mine, :] = send1[chunk, me]
+        if chunk == 0:
+            for copy in zeroth:
+                copy.wait()
+
+            @pl.when(inner)
+            def _():
+                relay(near, 2, 0).start()
+
+    @pl.when(inner)
+    def _():
+        relay(near, 2, 0).wait()
+        relay(away, 4, 1).start()
 
     column = lax.broadcasted_iota(jnp.int32, (length, 2 * length), 1)
     line = column // tile * rows_j + lax.rem(column, rows_j)
@@ -172,8 +200,14 @@
 
     lax.fori_loop(0, all_sources // 16, unpack_panel, 0)
 
-    for copy in zeroth:
-        copy.wait()
+    @pl.when(inner)
+    def _():
+        relay(away, 4, 1).wait_send()
+
+    @pl.when(jnp.logical_not(inner))
+    def _():
+        relay(away, 4, 1).wait_recv()
+
     for block in range(16):
         lo = block * 128
         weights[:, lo:lo + 128] = recv_op[:, lo:lo + 128].astype(jnp.float32) * (
@@ -249,18 +283,20 @@
     width = order.shape[0]
     if width > 8 * foci:
         pieces.append(jnp.zeros((width - 8 * foci, all_sources), jnp.float32))
-    total[...] = jnp.concatenate(pieces, 0).T
-
-    sources = recv3.shape[1]
+    sources = joined.shape[1]
+    total[...] = jnp.concatenate(pieces, 0).T.reshape(chips, 2, sources, width)
+    third = send(total.at[:, 1 - core], twin, parts - 2, sends3, recvs3)
+    third.wait()
+    for to in range(chips):
+        joined[to] = total[to, core] + twin[to]
     third = [
-        send(total.at[rows_of(other * 2 + side, sources), :], recv3.at[number], number,
-             sends3, recvs3)
-        for number, (other, side) in enumerate(peers)
+        send(joined.at[peers[number][0]], recv3.at[number // 2], number, sends3, recvs3)
+        for number in (0, 2, 4)
     ]
-    reflected = total[rows_of(me, sources), :]
-    for number, copy in enumerate(third):
+    reflected = joined[chip]
+    for copy in third:
         copy.wait()
-    for number in range(parts - 1):
+    for number in range(chips - 1):
         reflected = reflected + recv3[number]
 
     weight = (freq + 1).astype(jnp.float32) * (2.0 / (freqs * (freqs + 1)))
@@ -358,8 +394,10 @@
             pltpu.VMEM((parts * rows_j * 16, 128), jnp.float32),
             pltpu.VMEM((chunks, parts, 16, rows_j * 128), jnp.bfloat16),
             pltpu.VMEM((chunks, 2, chips * 16, rows_j * 128), jnp.bfloat16),
-            pltpu.VMEM((all_sources, width), jnp.float32),
-            pltpu.VMEM((parts - 1, sources, width), jnp.float32),
+            pltpu.VMEM((chips, 2, sources, width), jnp.float32),
+            pltpu.VMEM((chips, sources, width), jnp.float32),
+            pltpu.VMEM((chips, sources, width), jnp.float32),
+            pltpu.VMEM((chips - 1, sources, width), jnp.float32),
             pltpu.VMEM((freqs, 8, 128), jnp.float32),
             pair, pair, many, many, many, many, pair, pair,
             pltpu.SemaphoreType.DMA((freqs,)),
@@ -367,7 +405,7 @@
             pltpu.SemaphoreType.DMA((chunks + 1,)),
         ],
         compiler_params=pltpu.CompilerParams(
-            collective_id=0, has_side_effects=True, vmem_limit_bytes=48 * 1024 * 1024
+            collective_id=0, has_side_effects=True, vmem_limit_bytes=63 * 1024 * 1024
         ),
     )(
         live_count,

time: 73.9 us -> 67.8 us (0.917)
  local copies, waits for them, and re-layouts: 8.09 us -> 2.55 us
    unnamed x16 -> x2, local copies, waits for them, and re-layouts: 8.09 us -> 2.55 us
where the time goes in v3:
time: 67.8 us; the launch traced here: 67.6 us
  Pallas kernels  64.4 us (95%)
  local copies, waits for them, and re-layouts  2.55 us (4%)
    pallas_call x1, Pallas kernels, fused(): pl.pallas_call(lambda *refs: update_kernel(freqs, parts, foci, rows_j, *r...  64.4 us
    unnamed x2, local copies, waits for them, and re-layouts  2.55 us

profile of v3, /device:TPU:0, one launch (start us, length us, event | category | flops | bytes accessed | tf_op | source)
XLA Modules:
  0.0 67.6 jit_solution(260394266299568253)
XLA Ops:
  0.6 64.4 %shard_map.86 = (f32[32,2,96]{2,1,0:T(2,128)}, f32[1,32]{1,0:T(1,128)}) custom-call(s32[8]{0:T(128)} %refs_0_.1, s32[1,64]{1,0:T(1,128)} %bitcast.14, f32[2,4,4,3,2,8,256]{6,5,4,3,2,1,0:T(8,128)} %bitcast.10, f32[2,4,4,8,256]{4,3,2,1,0:T(8,128)} %bitcast.11, bf16[256,2,2048]{2,1,0:T(2,128)(2,1)} %bitcast.9, f32[32,2,96]{2,1,0:T(2,128)} %bitcast.12, ...), custom_call_target="tpu_custom_call" | custom-call | tf_op jit(solution)/shard_map/pallas_call | solution.py:376
  65.0 1.4 %copy.12 = f32[32,1,2,96]{3,2,1,0:T(2,128)} copy(f32[32,1,2,96]{3,2,1,0:T(2,128)} %bitcast.13) | data formatting | bytes 49152
  66.4 1.2 %copy.13 = f32[32]{0:T(128)} copy(f32[32]{0:T(128)} %bitcast.15) | data formatting | bytes 256
